TPU v7x, 512 devices: a whole 4x4x16 slice. The times are simulated.
512 devices in a mesh: ia: 16 (over z), ja: 8 (over y, core), ka: 4 (over x).
Axes of the slice: x: 4, y: 4, z: 16, core: 2. Of those that a mesh axis runs over, the one named last changes fastest.
Arguments:
- tensor_tiles: bfloat16 [16, 8, 4, 8, 64, 4096], P('ia', 'ja', 'ka'), may hold values from -6 to 6
- item_rows: bfloat16 [1024, 64, 128], P(('ia', 'ja')), may hold values from -0.75 to 0.75
- word_rows: bfloat16 [128, 64, 128], P(('ia', 'ka')), may hold values from -0.75 to 0.75
- heavy_local: int32 [16, 8, 1], P('ia', 'ja'), may hold values from 0 to 7
- send_blocks: int32 [16, 8, 4, 16, 1], P('ia', 'ja', 'ka'), may hold values from 0 to 7
- tile_slot: int32 [16, 8, 4, 8], P('ia', 'ja', 'ka'), may hold values from 0 to 31
- tile_word: int32 [16, 8, 4, 8], P('ia', 'ja', 'ka'), may hold values from 0 to 31
- tile_user: int32 [16, 8, 4, 8], P('ia', 'ja', 'ka'), may hold values from 0 to 31, as said below
- tile_count: int32 [16, 8, 4], P('ia', 'ja', 'ka'), may hold values from 1 to 8
Outputs:
- user_panel: float32 [512, 64, 128], P(('ia', 'ja', 'ka'))
Inputs may be any that keep to these rules, and one draw needn't show every extreme that they name: The tiles of one device name different user blocks: tile_user differs between any two tiles of one device.
All inputs are finite; a program needn't handle non-finite values.
Results may differ from a plain program's by a relative error of at most 0.0029.
Values may be sent and summed in bfloat16 or wider, within the bound.
A program may use at most 64 MiB of HBM per device.

v0:
```python
import jax
import jax.numpy as jnp
from jax import lax
from jax.sharding import PartitionSpec as P

UB_DEV = 1


def local(
    tensor_tiles,
    item_rows,
    word_rows,
    heavy_local,
    send_blocks,
    tile_slot,
    tile_word,
    tile_user,
    tile_count,
):
    peer_count = lax.axis_size("ia")
    tile_edge = item_rows.shape[1]
    rank_cols = item_rows.shape[2]
    slot_count = send_blocks.shape[-1]
    tiles_local = tensor_tiles.reshape(tensor_tiles.shape[3:])
    tiles_count = tiles_local.shape[0]
    slots_here = tile_slot.reshape(-1)
    heavy_here = heavy_local.reshape(-1)
    send_here = send_blocks.reshape(peer_count, slot_count)
    words = lax.all_gather(word_rows, "ia", axis=0, tiled=True)
    heavy = jnp.take(item_rows, heavy_here, axis=0)
    heavy_all = lax.all_gather(heavy, "ia", axis=0, tiled=True)
    outgoing = jnp.take(item_rows, send_here.reshape(-1), axis=0).reshape(
        peer_count, slot_count, tile_edge, rank_cols
    )
    incoming = lax.all_to_all(outgoing, "ia", split_axis=0, concat_axis=0, tiled=True)
    table = jnp.concatenate([heavy_all, incoming.reshape(-1, tile_edge, rank_cols)], axis=0)
    item_tile = jnp.take(table, slots_here, axis=0)
    word_tile = jnp.take(words, tile_word.reshape(-1), axis=0)
    krao = (
        item_tile.astype(jnp.float32)[:, :, None, :] * word_tile.astype(jnp.float32)[:, None, :, :]
    ).astype(jnp.bfloat16)
    krao = krao.reshape(tiles_count, tile_edge * tile_edge, rank_cols)
    contrib = jnp.einsum("tab,tbr->tar", tiles_local, krao, preferred_element_type=jnp.float32)
    live = (jnp.arange(tiles_count) < tile_count.reshape(())).astype(jnp.float32)
    contrib = contrib * live[:, None, None]
    owner_total = lax.axis_size("ja") * lax.axis_size("ka")
    users_here = tile_user.reshape(-1)
    user_blocks = UB_DEV * owner_total
    onehot = (users_here[None, :] == jnp.arange(user_blocks)[:, None]).astype(jnp.float32)
    partial_rows = jnp.einsum("ut,tar->uar", onehot, contrib, precision=lax.Precision.HIGHEST)
    return lax.psum_scatter(partial_rows, ("ja", "ka"), scatter_dimension=0, tiled=True)


def solution(mesh):
    return jax.shard_map(
        local,
        mesh=mesh,
        in_specs=(
            P("ia", "ja", "ka", None, None, None),
            P(("ia", "ja"), None, None),
            P(("ia", "ka"), None, None),
            P("ia", "ja", None),
            P("ia", "ja", "ka", None, None),
            P("ia", "ja", "ka", None),
            P("ia", "ja", "ka", None),
            P("ia", "ja", "ka", None),
            P("ia", "ja", "ka"),
        ),
        out_specs=P(("ia", "ja", "ka"), None, None),
        check_vma=False,
    )
```

profile of v0, /device:TPU:1, one launch (start us, length us, event | category | flops | bytes accessed | tf_op | source)
XLA Modules:
  0.0 210.9 jit_solution(4341602793392673329)
XLA Ops:
  6.5 0.7 fusion.8
  7.2 0.7 compare_and_fusion.2
  7.9 1.5 gather_fusion
  9.4 0.8 bitcast_select_fusion
  10.2 15.7 %all-to-all-start = ((bf16[16,1,64,128]{3,2,1,0:T(8,128)(2,1)}), bf16[16,1,64,128]{3,2,1,0:T(8,128)(2,1)S(1)}, u32[]{:S(2)}, u32[]{:S(2)}) async-start(bf16[16,1,64,128]{3,2,1,0:T(8,128)(2,1)} %bitcast_select_fusion), calls=%async_computation | async-start | bytes 524288 | tf_op jit(solution)/shard_map/all_to_all | solution.py:35
  25.9 0.0 reduce-scatter.2.cloned.1.call-start
  26.6 0.7 compare_select_fusion.1
  27.3 33.8 %all_gather.7 = bf16[32,64,128]{2,1,0:T(8,128)(2,1)S(1)} all-gather(bf16[2,64,128]{2,1,0:T(8,128)(2,1)} %param.13), channel_id=1, replica_groups=mesh['ia'=16,'ja'=8,'ka'=4] {'ia'}, dimensions={0}, use_global_device_ids=true | all-gather | bytes 557056 | tf_op jit(solution)/shard_map/all_gather | solution.py:29
  61.1 0.7 compare_select_fusion
  62.4 0.6 gather_fusion.2
  63.0 0.7 dynamic-slice_select_fusion
  63.7 20.7 %all_gather.6 = bf16[16,64,128]{2,1,0:T(8,128)(2,1)S(1)} all-gather(bf16[1,64,128]{2,1,0:T(8,128)(2,1)S(1)} %dynamic-slice_select_fusion), channel_id=1, replica_groups=mesh['ia'=16,'ja'=8,'ka'=4] {'ia'}, dimensions={0}, use_global_device_ids=true | all-gather | bytes 278528 | tf_op jit(solution)/shard_map/all_gather | solution.py:31
  84.4 0.7 compare_and_fusion.1
  85.0 0.7 compare_and_fusion
  85.7 0.1 select_convert_fusion
  85.8 0.0 all-to-all-done
  85.9 0.6 gather_fusion.1
  86.5 0.0 copy-start
  86.5 0.1 select_convert_fusion.1
  86.6 2.4 %multiply_convert_fusion = bf16[8,64,64,128]{3,2,1,0:T(8,128)(2,1)S(1)} fusion(f32[8,64,128]{2,1,0:T(8,128)S(1)} %select_convert_fusion, f32[8,64,128]{2,1,0:T(8,128)S(1)} %select_convert_fusion.1), kind=kLoop, calls=%fused_computation.3 | loop fusion | flops 8388608 | bytes 8912896 | tf_op jit(solution)/shard_map/convert_element_type | solution.py:41
  88.9 0.0 copy-start.1
  89.0 0.0 copy-done
  89.0 1.6 fusion
  90.5 0.0 copy-done.1
  90.6 0.7 fusion.2
  91.2 1.6 copy.11
  92.8 0.0 reduce-scatter.2.cloned.1.call-update
  92.9 111.2 %reduce-scatter.2.cloned.1.call-done = f32[1,64,128]{2,1,0:T(8,128)} async-done(((f32[32,64,128]{2,1,0:T(8,128)}), f32[1,64,128]{2,1,0:T(8,128)}) %reduce-scatter.2.cloned.1.call-update) | async-done | bytes 32784 | tf_op jit(solution)/shard_map/reduce_scatter | solution.py:51
  (5 shorter events, 0.1 us)
Async XLA Ops:
  10.2 75.7 %all-to-all-start = ((bf16[16,1,64,128]{3,2,1,0:T(8,128)(2,1)}), bf16[16,1,64,128]{3,2,1,0:T(8,128)(2,1)S(1)}, u32[]{:S(2)}, u32[]{:S(2)}) async-start(bf16[16,1,64,128]{3,2,1,0:T(8,128)(2,1)} %bitcast_select_fusion), calls=%async_computation | async-start | bytes 524288 | tf_op jit(solution)/shard_map/all_to_all | solution.py:35
  25.9 178.1 %reduce-scatter.2.cloned.1.call-start = ((), (), s32[]{:S(2)}) async-start(), calls=%async_computation.2 | async-start | bytes 1081344 | tf_op jit(solution)/shard_map/reduce_scatter | solution.py:51
  86.5 2.5 %copy-start = (bf16[1,1,1,8,64,4096]{5,4,3,2,1,0:T(8,128)(2,1)S(1)}, bf16[1,1,1,8,64,4096]{5,4,3,2,1,0:T(8,128)(2,1)}, u32[]{:S(2)}) copy-start(bf16[1,1,1,8,64,4096]{5,4,3,2,1,0:T(8,128)(2,1)} %param.11) | copy-start | bytes 12582916
  88.9 1.6 copy-start.1
Sparse Core Ops, SparseCore 0:
  93.0 111.0 reduce-scatter.1
where the time goes:
time: 212 us; the launch traced here: 211 us
  waiting for transfers between devices  111 us (52%)
  blocking collectives  54.5 us (26%)
  starting transfers between devices  15.8 us (7%)
  between operations  14.8 us (7%)
  other arithmetic  8.1 us (4%)
  local copies, waits for them, and re-layouts  4.24 us (2%)
  matrix products  2.26 us (1%)
    reduce_scatter x1, waiting for transfers between devices, local(): lax.psum_scatter(partial_rows, ('ja', 'ka'), scatter_dimension=0, tiled=T...  111 us
    all_gather x1, blocking collectives, local(): words = lax.all_gather(word_rows, 'ia', axis=0, tiled=True)  33.8 us
    all_gather x1, blocking collectives, local(): heavy_all = lax.all_gather(heavy, 'ia', axis=0, tiled=True)  20.7 us
    all_to_all x1, starting transfers between devices, local(): lax.all_to_all(outgoing, 'ia', split_axis=0, concat_axis=0, tiled=True)  15.7 us
  transfers between devices with their start and end apart: 2, of which 1 were waited for; matrix products, arithmetic and copies ran while one was open for 2% of the time, Pallas kernels for 0%

commit v1 on v0

v1 whole, which is shorter than its diff:
```python
import functools

import jax
import jax.numpy as jnp
from jax import lax
from jax.experimental import pallas as pl
from jax.experimental.pallas import tpu as pltpu
from jax.sharding import PartitionSpec as P

MESH = pl.DeviceIdType.MESH
NZ, NX, NY, NC = 16, 4, 4, 2
TILES = 8
E = 64
R = 128
Q = E // NX
BF = jnp.bfloat16
F32 = jnp.float32
Z_ORDER = (8, 7, 9, 6, 10, 5, 11, 4, 12, 3, 13, 2, 14, 1, 15)


def remote(src, dst, send_sem, recv_sem, device):
    return pltpu.make_async_remote_copy(
        src_ref=src, dst_ref=dst, send_sem=send_sem, recv_sem=recv_sem, device_id=device, device_id_type=MESH
    )


def kernel(
    tiles_hbm, item_hbm, word_hbm, heavy_hbm, send_hbm, slot_hbm, tword_hbm, user_hbm, count_hbm,
    out_ref,
    tiles, items, gath, table, words, light, item32, krao, contrib, pair_out, pair_in, plane_out, plane_in, own,
    heavy_s, send_s, slot_s, tword_s, user_s, count_s, inv_s,
    tile_sem, load_sem, int_sem,
    zg_send, zg_recv, zl_send, zl_recv, x_send, x_recv, y_send, y_recv, c_send, c_recv, p_send, p_recv, q_send, q_recv,
):
    i = lax.axis_index("ia")
    j = lax.axis_index("ja")
    k = lax.axis_index("ka")
    y = j // 2
    c = lax.rem(j, 2)
    chip = y * NX + k

    def zpeer(d):
        return lax.rem(i + d, NZ)

    def chip_dev(q):
        return {"ja": (q // NX) * 2 + c, "ka": lax.rem(q, NX)}

    other = {"ja": y * 2 + 1 - c}

    ints = [
        pltpu.make_async_copy(a, b, int_sem.at[n])
        for n, (a, b) in enumerate(
            (
                (heavy_hbm, heavy_s), (send_hbm, send_s), (slot_hbm, slot_s),
                (tword_hbm, tword_s), (user_hbm, user_s), (count_hbm, count_s),
            )
        )
    ]
    for cp in ints:
        cp.start()
    load_items = pltpu.make_async_copy(item_hbm, items, load_sem.at[0])
    load_items.start()
    kq = pl.multiple_of(k * Q, Q)
    yq = pl.multiple_of(y * Q, Q)
    load_word = pltpu.make_async_copy(word_hbm.at[c, pl.ds(yq, Q)], gath.at[i, 1], load_sem.at[1])
    load_word.start()

    barrier = pltpu.get_barrier_semaphore()
    for d in Z_ORDER:
        pl.semaphore_signal(barrier, inc=1, device_id={"ia": zpeer(d)}, device_id_type=MESH)
    for d in range(1, 16):
        pl.semaphore_signal(barrier, inc=1, device_id=chip_dev(lax.rem(chip + d, 16)), device_id_type=MESH)
    pl.semaphore_signal(barrier, inc=1, device_id=other, device_id_type=MESH)

    tile_loads = [pltpu.make_async_copy(tiles_hbm.at[0, 0, 0, t], tiles.at[t], tile_sem.at[t]) for t in range(TILES)]
    for cp in tile_loads:
        cp.start()

    for cp in ints:
        cp.wait()
    load_items.wait()
    load_word.wait()
    gath[i, 0] = items[heavy_s[0, 0, 0], pl.ds(kq, Q), :]
    for p in range(NZ):
        light[p] = items[send_s[0, 0, 0, p]]
    table[NZ + i] = items[send_s[0, 0, 0, i]]

    count = count_s[0, 0, 0]

    def find(u, carry):
        at = jnp.int32(TILES)
        for t in range(TILES):
            at = jnp.where((user_s[0, 0, 0, t] == u) & (count > t), t, at)
        inv_s[u] = at
        return carry

    lax.fori_loop(0, NX * NY * NC, find, 0)
    contrib[TILES] = jnp.zeros((E, R), F32)

    pl.semaphore_wait(barrier, 31)

    zg = [
        remote(gath.at[i], gath.at[i], zg_send.at[d], zg_recv.at[d], {"ia": zpeer(d)}) for d in Z_ORDER
    ]
    for cp in zg:
        cp.start()
    zl = [
        remote(light.at[zpeer(d)], table.at[NZ + i], zl_send.at[d], zl_recv.at[d], {"ia": zpeer(d)}) for d in Z_ORDER
    ]
    for cp in zl:
        cp.start()

    for cp in zg:
        cp.wait_recv()
    xs = [
        remote(gath.at[:, 0], table.at[pl.ds(0, NZ), pl.ds(kq, Q)], x_send.at[d], x_recv.at[d], {"ka": lax.rem(k + d, NX)})
        for d in (2, 1, 3)
    ]
    ys = [
        remote(gath.at[:, 1], words.at[:, c, pl.ds(yq, Q)], y_send.at[d], y_recv.at[d], {"ja": lax.rem(j + 2 * d, 8)})
        for d in (2, 1, 3)
    ]
    for a, b in zip(xs, ys):
        a.start()
        b.start()
    for p in range(NZ):
        table[p, pl.ds(kq, Q), :] = gath[p, 0]
        words[p, c, pl.ds(yq, Q), :] = gath[p, 1]
    for cp in ys:
        cp.wait_recv()
    cx = remote(words.at[:, c], words.at[:, c], c_send.at[0], c_recv.at[0], other)
    cx.start()
    for cp in xs:
        cp.wait_recv()
    for cp in zl:
        cp.wait_recv()
    cx.wait_recv()
    for cp in tile_loads:
        cp.wait()

    def one_tile(t, carry):
        item32[...] = table[slot_s[0, 0, 0, t]].astype(F32)
        q = tword_s[0, 0, 0, t]
        word = words[q >> 1, q & 1]
        for b in range(E):
            row = jnp.broadcast_to(item32[pl.ds(b, 1), :], (E, R)).astype(BF)
            krao[pl.ds(b * E, E), :] = row * word
        contrib[t] = jnp.dot(tiles[t], krao[...], preferred_element_type=F32)
        return carry

    lax.fori_loop(0, TILES, one_tile, 0)

    def to_pair(q, carry):
        pair_out[q] = contrib[inv_s[(q // NX) * 8 + (1 - c) * NX + lax.rem(q, NX)]].astype(BF)
        return carry

    lax.fori_loop(0, 16, to_pair, 0)
    px = remote(pair_out, pair_in, p_send.at[0], p_recv.at[0], other)
    px.start()
    px.wait_recv()

    for d in range(1, 16):
        q = lax.rem(chip + d, 16)
        mine = contrib[inv_s[(q // NX) * 8 + c * NX + lax.rem(q, NX)]]
        plane_out[q] = (mine + pair_in[q].astype(F32)).astype(BF)
        remote(plane_out.at[q], plane_in.at[d], q_send.at[d], q_recv.at[d], chip_dev(q)).start()
    own[...] = contrib[inv_s[y * 8 + c * NX + k]] + pair_in[chip].astype(F32)

    for d in range(1, 16):
        q = lax.rem(chip + d, 16)
        remote(plane_out.at[q], plane_in.at[d], q_send.at[d], q_recv.at[d], chip_dev(q)).wait_recv()
        own[...] += plane_in[d].astype(F32)
    out_ref[0] = own[...]

    for cp in zg + zl + xs + ys + [cx, px]:
        cp.wait_send()
    for d in range(1, 16):
        q = lax.rem(chip + d, 16)
        remote(plane_out.at[q], plane_in.at[d], q_send.at[d], q_recv.at[d], chip_dev(q)).wait_send()


def local(*args):
    args = list(args)
    args[4] = args[4].reshape(1, 1, 1, NZ)
    dma = pltpu.SemaphoreType.DMA
    return pl.pallas_call(
        kernel,
        out_shape=jax.ShapeDtypeStruct((1, E, R), F32),
        in_specs=[pl.BlockSpec(memory_space=pltpu.HBM)] * 9,
        out_specs=pl.BlockSpec(memory_space=pltpu.VMEM),
        scratch_shapes=[
            pltpu.VMEM((TILES, E, E * E), BF),
            pltpu.VMEM((8, E, R), BF),
            pltpu.VMEM((NZ, 2, Q, R), BF),
            pltpu.VMEM((2 * NZ, E, R), BF),
            pltpu.VMEM((NZ, 2, E, R), BF),
            pltpu.VMEM((NZ, E, R), BF),
            pltpu.VMEM((E, R), F32),
            pltpu.VMEM((E * E, R), BF),
            pltpu.VMEM((TILES + 1, E, R), F32),
            pltpu.VMEM((16, E, R), BF),
            pltpu.VMEM((16, E, R), BF),
            pltpu.VMEM((16, E, R), BF),
            pltpu.VMEM((16, E, R), BF),
            pltpu.VMEM((E, R), F32),
            pltpu.SMEM((1, 1, 1), jnp.int32),
            pltpu.SMEM((1, 1, 1, NZ), jnp.int32),
            pltpu.SMEM((1, 1, 1, TILES), jnp.int32),
            pltpu.SMEM((1, 1, 1, TILES), jnp.int32),
            pltpu.SMEM((1, 1, 1, TILES), jnp.int32),
            pltpu.SMEM((1, 1, 1), jnp.int32),
            pltpu.SMEM((32,), jnp.int32),
            dma((TILES,)), dma((2,)), dma((6,)),
            dma((16,)), dma((16,)), dma((16,)), dma((16,)),
            dma((4,)), dma((4,)), dma((4,)), dma((4,)),
            dma((1,)), dma((1,)), dma((1,)), dma((1,)),
            dma((16,)), dma((16,)),
        ],
        compiler_params=pltpu.CompilerParams(collective_id=0, has_side_effects=True, vmem_limit_bytes=32 << 20),
        name="mttkrp",
    )(*args)


def solution(mesh):
    return jax.shard_map(
        local,
        mesh=mesh,
        in_specs=(
            P("ia", "ja", "ka", None, None, None),
            P(("ia", "ja"), None, None),
            P(("ia", "ka"), None, None),
            P("ia", "ja", None),
            P("ia", "ja", "ka", None, None),
            P("ia", "ja", "ka", None),
            P("ia", "ja", "ka", None),
            P("ia", "ja", "ka", None),
            P("ia", "ja", "ka"),
        ),
        out_specs=P(("ia", "ja", "ka"), None, None),
        check_vma=False,
    )
```

time: 212 us -> 56.7 us (0.27)
  waiting for transfers between devices: 111 us -> 0 us
  blocking collectives: 54.5 us -> 0 us
  Pallas kernels: 0 us -> 48 us
  starting transfers between devices: 15.8 us -> 0 us
  between operations: 14.8 us -> 1.32 us
  other arithmetic: 8.1 us -> 0 us
  local copies, waits for them, and re-layouts: 4.24 us -> 7.08 us
  matrix products: 2.26 us -> 0 us
    reduce_scatter x1 -> x0, waiting for transfers between devices: 111 us -> none  [local(): lax.psum_scatter(partial_rows, ('ja', 'ka'), scatter_dimension=0, tiled=T...]
    all_gather x2 -> x0, blocking collectives: 54.5 us -> none  [the longest x1 33.8 us: local(): words = lax.all_gather(word_rows, 'ia', axis=0, tiled=True)]
    pallas_call x0 -> x1, Pallas kernels: none -> 48 us  [local(): pl.pallas_call(kernel, out_shape=jax.ShapeDtypeStruct((1, E, R), F32), in...]
    all_to_all x1 -> x0, starting transfers between devices: 15.7 us -> none  [local(): lax.all_to_all(outgoing, 'ia', split_axis=0, concat_axis=0, tiled=True)]
    unnamed x4 -> x15, local copies, waits for them, and re-layouts: 0.01 us -> 7.08 us
    select_n x5 -> x0, other arithmetic: 3.49 us -> none  [the longest x2 1.44 us: local(): jnp.take(item_rows, send_here.reshape(-1), axis=0)]
    gather x3 -> x0, local copies, waits for them, and re-layouts: 2.65 us -> none  [the longest x1 1.5 us: local(): jnp.take(item_rows, send_here.reshape(-1), axis=0)]
    convert_element_type x4 -> x0, other arithmetic: 2.55 us -> none  [the longest x1 2.37 us: local(): krao = (item_tile.astype(jnp.float32)[:, :, None, :] * word_tile.astype(j...]
  transfers between devices with their start and end apart: 2 -> 0, of which waited for: 1 -> 0; matrix products, arithmetic and copies ran while one was open for 2% -> 0% of each run, Pallas kernels for 0% -> 0%
where the time goes in v1:
time: 56.7 us; the launch traced here: 56.4 us
  Pallas kernels  48 us (85%)
  local copies, waits for them, and re-layouts  7.08 us (12%)
  between operations  1.32 us (2%)
    pallas_call x1, Pallas kernels, local(): pl.pallas_call(kernel, out_shape=jax.ShapeDtypeStruct((1, E, R), F32), in...  48 us
    unnamed x15, local copies, waits for them, and re-layouts  7.08 us

profile of v1, /device:TPU:1, one launch (start us, length us, event | category | flops | bytes accessed | tf_op | source)
XLA Modules:
  0.0 56.4 jit_solution(10068590409099884440)
XLA Ops:
  1.3 0.0 copy-start
  1.3 2.2 %copy-done = bf16[1,1,1,8,64,4096]{5,4,3,2,1,0:T(8,128)(2,1)S(1)} copy-done((bf16[1,1,1,8,64,4096]{5,4,3,2,1,0:T(8,128)(2,1)S(1)}, bf16[1,1,1,8,64,4096]{5,4,3,2,1,0:T(8,128)(2,1)}, u32[]{:S(2)}) %copy-start) | copy-done | bytes 4194328
  3.5 0.0 copy-start.1
  3.5 0.9 %copy-done.1 = bf16[8,64,128]{2,1,0:T(8,128)(2,1)S(1)} copy-done((bf16[8,64,128]{2,1,0:T(8,128)(2,1)S(1)}, bf16[8,64,128]{2,1,0:T(8,128)(2,1)}, u32[]{:S(2)}) %copy-start.1) | copy-done | bytes 131096
  4.4 0.0 copy-start.2
  4.4 0.8 %copy-done.2 = bf16[2,64,128]{2,1,0:T(8,128)(2,1)S(1)} copy-done((bf16[2,64,128]{2,1,0:T(8,128)(2,1)S(1)}, bf16[2,64,128]{2,1,0:T(8,128)(2,1)}, u32[]{:S(2)}) %copy-start.2) | copy-done | bytes 32792
  5.1 0.0 copy-start.3
  5.2 0.7 %copy-done.3 = s32[1,1,1,16,1]{3,4,2,1,0:T(1,128)S(1)} copy-done((s32[1,1,1,16,1]{3,4,2,1,0:T(1,128)S(1)}, s32[1,1,1,16,1]{3,4,2,1,0:T(1,128)}, u32[]{:S(2)}) %copy-start.3) | copy-done | bytes 88
  5.8 0.0 copy-start.4
  5.8 0.7 %copy-done.4 = s32[1,1,1,8]{3,2,1,0:T(1,128)S(1)} copy-done((s32[1,1,1,8]{3,2,1,0:T(1,128)S(1)}, s32[1,1,1,8]{3,2,1,0:T(1,128)}, u32[]{:S(2)}) %copy-start.4) | copy-done | bytes 56
  6.5 0.0 copy-start.5
  6.5 0.7 %copy-done.5 = s32[1,1,1,8]{3,2,1,0:T(1,128)S(1)} copy-done((s32[1,1,1,8]{3,2,1,0:T(1,128)S(1)}, s32[1,1,1,8]{3,2,1,0:T(1,128)}, u32[]{:S(2)}) %copy-start.5) | copy-done | bytes 56
  7.1 0.0 copy-start.6
  7.1 0.7 %copy-done.6 = s32[1,1,1,8]{3,2,1,0:T(1,128)S(1)} copy-done((s32[1,1,1,8]{3,2,1,0:T(1,128)S(1)}, s32[1,1,1,8]{3,2,1,0:T(1,128)}, u32[]{:S(2)}) %copy-start.6) | copy-done | bytes 56
  7.8 48.0 %mttkrp.1 = f32[1,64,128]{2,1,0:T(8,128)S(1)} custom-call(bf16[1,1,1,8,64,4096]{5,4,3,2,1,0:T(8,128)(2,1)S(1)} %copy-done, bf16[8,64,128]{2,1,0:T(8,128)(2,1)S(1)} %copy-done.1, bf16[2,64,128]{2,1,0:T(8,128)(2,1)S(1)} %copy-done.2, s32[1,1,1]{2,1,0:T(1,128)S(6)} %copy.11.heavy_hbm, s32[1,1,1,16]{3,2,1,0:T(1,128)S(1)} %bitcast.1, ...), custom_call_target="tpu_custom_call" | custom-call | tf_op jit(solution)/shard_map/mttkrp/pallas_call | solution.py:186
  55.8 0.6 %copy.13 = f32[1,64,128]{2,1,0:T(8,128)} copy(f32[1,64,128]{2,1,0:T(8,128)S(1)} %mttkrp.1) | data formatting | bytes 65536
Async XLA Ops:
  1.3 2.2 %copy-start = (bf16[1,1,1,8,64,4096]{5,4,3,2,1,0:T(8,128)(2,1)S(1)}, bf16[1,1,1,8,64,4096]{5,4,3,2,1,0:T(8,128)(2,1)}, u32[]{:S(2)}) copy-start(bf16[1,1,1,8,64,4096]{5,4,3,2,1,0:T(8,128)(2,1)} %tiles_hbm.1) | copy-start | bytes 12582916
  3.5 0.9 %copy-start.1 = (bf16[8,64,128]{2,1,0:T(8,128)(2,1)S(1)}, bf16[8,64,128]{2,1,0:T(8,128)(2,1)}, u32[]{:S(2)}) copy-start(bf16[8,64,128]{2,1,0:T(8,128)(2,1)} %item_hbm.1) | copy-start | bytes 393220
  4.4 0.8 %copy-start.2 = (bf16[2,64,128]{2,1,0:T(8,128)(2,1)S(1)}, bf16[2,64,128]{2,1,0:T(8,128)(2,1)}, u32[]{:S(2)}) copy-start(bf16[2,64,128]{2,1,0:T(8,128)(2,1)} %word_hbm.1) | copy-start | bytes 98308
  5.1 0.7 %copy-start.3 = (s32[1,1,1,16,1]{3,4,2,1,0:T(1,128)S(1)}, s32[1,1,1,16,1]{3,4,2,1,0:T(1,128)}, u32[]{:S(2)}) copy-start(s32[1,1,1,16,1]{3,4,2,1,0:T(1,128)} %param.13) | copy-start | bytes 196
  5.8 0.7 %copy-start.4 = (s32[1,1,1,8]{3,2,1,0:T(1,128)S(1)}, s32[1,1,1,8]{3,2,1,0:T(1,128)}, u32[]{:S(2)}) copy-start(s32[1,1,1,8]{3,2,1,0:T(1,128)} %slot_hbm.1) | copy-start | bytes 100
  6.5 0.7 %copy-start.5 = (s32[1,1,1,8]{3,2,1,0:T(1,128)S(1)}, s32[1,1,1,8]{3,2,1,0:T(1,128)}, u32[]{:S(2)}) copy-start(s32[1,1,1,8]{3,2,1,0:T(1,128)} %tword_hbm.1) | copy-start | bytes 100
  7.1 0.7 %copy-start.6 = (s32[1,1,1,8]{3,2,1,0:T(1,128)S(1)}, s32[1,1,1,8]{3,2,1,0:T(1,128)}, u32[]{:S(2)}) copy-start(s32[1,1,1,8]{3,2,1,0:T(1,128)} %user_hbm.1) | copy-start | bytes 100

commit v2 on v1

v2 whole, which is shorter than its diff:
```python
import jax
import jax.numpy as jnp
from jax import lax
from jax.experimental import pallas as pl
from jax.experimental.pallas import tpu as pltpu
from jax.sharding import PartitionSpec as P

MESH = pl.DeviceIdType.MESH
NZ, NX, NY, NC = 16, 4, 4, 2
TILES = 8
E = 64
R = 128
Q = E // NX
H = E // 2
BF = jnp.bfloat16
F32 = jnp.float32
NEAR = (0, 1, 15, 2, 14, 4, 12)
FAR = (3, 13, 5, 11, 6, 10, 7, 9, 8)
POS = {r: n for n, r in enumerate(NEAR + FAR)}
SPLIT = len(NEAR)
HEAVY, COUNT = 0, 1


def kernel(
    tiles_hbm, item_hbm, word_hbm, pair_hbm, send_hbm, slot_hbm, tword_hbm, user_hbm,
    out_ref,
    tiles, items, gath, table, words, light, relay, item32, krao_a, krao_b, contrib, pcontrib, plane_out, plane_in,
    pair_s, send_s, slot_s, tword_s, user_s, ppair_s, puser_s, pos_s, inv_s, pinv_s,
    tile_sem, load_sem, ss, rs, t_send, t_recv, q_send, q_recv,
):
    i = lax.axis_index("ia")
    j = lax.axis_index("ja")
    k = lax.axis_index("ka")
    y = j // 2
    c = lax.rem(j, 2)
    chip = y * NX + k
    kq = pl.multiple_of(k * Q, Q)
    yq = pl.multiple_of(y * Q, Q)

    def zdev(d):
        return {"ia": lax.rem(i + (d % NZ), NZ)}

    def chip_dev(q):
        return {"ja": (q // NX) * 2 + c, "ka": lax.rem(q, NX)}

    other = {"ja": y * 2 + 1 - c}
    used = [0]

    def remote(src, dst, device):
        n = used[0]
        used[0] += 1
        return pltpu.make_async_remote_copy(
            src_ref=src, dst_ref=dst, send_sem=ss.at[n], recv_sem=rs.at[n], device_id=device, device_id_type=MESH
        )

    load_items = pltpu.make_async_copy(item_hbm, items, load_sem.at[0])
    load_word = pltpu.make_async_copy(word_hbm.at[c, pl.ds(yq, Q)], gath.at[0, 1], load_sem.at[1])
    ints = ((pair_hbm, pair_s), (send_hbm, send_s), (slot_hbm, slot_s), (tword_hbm, tword_s), (user_hbm, user_s))
    ints = [pltpu.make_async_copy(a, b, load_sem.at[2 + n]) for n, (a, b) in enumerate(ints)]
    for cp in ints:
        cp.start()
    load_items.start()
    load_word.start()

    barrier = pltpu.get_barrier_semaphore()
    for d in (4, -4, 3, -3, 2, -2, 1, -1):
        pl.semaphore_signal(barrier, inc=1, device_id=zdev(d), device_id_type=MESH)
    for d in range(1, 16):
        pl.semaphore_signal(barrier, inc=1, device_id=chip_dev(lax.rem(chip + d, 16)), device_id_type=MESH)
    pl.semaphore_signal(barrier, inc=1, device_id=other, device_id_type=MESH)

    tile_loads = [pltpu.make_async_copy(tiles_hbm.at[0, 0, 0, t], tiles.at[t], tile_sem.at[t]) for t in range(TILES)]
    for cp in tile_loads:
        cp.start()
    for r, n in POS.items():
        pos_s[r] = n

    for cp in ints:
        cp.wait()
    load_items.wait()
    load_word.wait()
    gath[0, 0] = items[pair_s[0, HEAVY], pl.ds(kq, Q), :]
    for d in range(1, NZ):
        light[d] = items[send_s[0, 0, 0, lax.rem(i + d, NZ)]]
    table[NZ] = items[send_s[0, 0, 0, i]]

    def find(pair, user, inv):
        count = pair[0, COUNT]

        def body(n, carry):
            u = (n // NX) * (NC * NX) + c * NX + lax.rem(n, NX)
            at = jnp.int32(TILES)
            for t in range(TILES):
                at = jnp.where((user[0, 0, 0, t] == u) & (count > t), t, at)
            inv[n] = at
            return carry

        lax.fori_loop(0, NX * NY, body, 0)

    find(pair_s, user_s, inv_s)
    contrib[TILES] = jnp.zeros((E, R), F32)
    pcontrib[TILES] = jnp.zeros((E, R), F32)

    pl.semaphore_wait(barrier, 24)

    def direct(d):
        return remote(gath.at[0], gath.at[POS[-d % NZ]], zdev(d))

    ag = {-d % NZ: direct(d) for d in (4, -4, 2, -2, 1, -1)}
    for cp in ag.values():
        cp.start()

    up = [remote(light.at[8, pl.ds(0, H)], relay.at[0, 3, pl.ds(0, H)], zdev(4))]
    down = [remote(light.at[8, pl.ds(H, H)], relay.at[1, 3, pl.ds(H, H)], zdev(-4))]
    for f in (3, 2, 1):
        up.append(remote(light.at[4 + f], relay.at[0, f - 1], zdev(4)))
        down.append(remote(light.at[NZ - 4 - f], relay.at[1, f - 1], zdev(-4)))
    for a, b in zip(up, down):
        a.start()
        b.start()
    px = [remote(pair_hbm, ppair_s, other), remote(user_hbm, puser_s, other)]
    for cp in px:
        cp.start()

    ag[12].wait_recv()
    ag[4].wait_recv()
    hops = [
        remote(gath.at[POS[12], 0], gath.at[POS[8], 0], zdev(4)),
        remote(gath.at[POS[4], 1], gath.at[POS[8], 1], zdev(-4)),
    ]
    for f in (3, 2, 1):
        hops.append(remote(gath.at[POS[12]], gath.at[POS[12 - f]], zdev(f)))
        hops.append(remote(gath.at[POS[4]], gath.at[POS[4 + f]], zdev(-f)))
    hops.append(remote(gath.at[POS[12]], gath.at[POS[13]], zdev(-1)))
    hops.append(remote(gath.at[POS[4]], gath.at[POS[3]], zdev(1)))
    for cp in hops:
        cp.start()

    near = [remote(light.at[d % NZ], table.at[NZ + (-d % NZ)], zdev(d)) for d in (4, -4, 3, -3, 2, -2, 1, -1)]
    for cp in near:
        cp.start()

    def spread(lo, n):
        out = []
        for d in (2, 1, 3):
            out.append(
                remote(
                    gath.at[pl.ds(lo, n), 1], words.at[pl.ds(lo, n), c, pl.ds(yq, Q)], {"ja": lax.rem(j + 2 * d, NY * NC)}
                )
            )
            out.append(
                remote(gath.at[pl.ds(lo, n), 0], table.at[pl.ds(lo, n), pl.ds(kq, Q)], {"ka": lax.rem(k + d, NX)})
            )
        for cp in out:
            cp.start()
        for n in range(lo, lo + n):
            table[n, pl.ds(kq, Q), :] = gath[n, 0]
            words[n, c, pl.ds(yq, Q), :] = gath[n, 1]
        return out

    for r in (14, 2, 15, 1):
        ag[r].wait_recv()
    spread_a = spread(0, SPLIT)

    fwd = []
    for n, f in enumerate((4, 3, 2, 1)):
        rows = (pl.ds(0, H), pl.ds(H, H)) if f == 4 else (pl.ds(0, E), pl.ds(0, E))
        up[n].wait_recv()
        fwd.append(remote(relay.at[0, f - 1, rows[0]], table.at[NZ + 12 - f, rows[0]], zdev(f)))
        fwd[-1].start()
        down[n].wait_recv()
        fwd.append(remote(relay.at[1, f - 1, rows[1]], table.at[NZ + 4 + f, rows[1]], zdev(-f)))
        fwd[-1].start()

    for cp in hops:
        cp.wait_recv()
    spread_b = spread(SPLIT, NZ - SPLIT)

    def pair_words(sent, lo, n):
        for cp in sent[0::2]:
            cp.wait_recv()
        cp = remote(words.at[pl.ds(lo, n), c], words.at[pl.ds(lo, n), c], other)
        cp.start()
        return cp

    pw = [pair_words(spread_a, 0, SPLIT), pair_words(spread_b, SPLIT, NZ - SPLIT)]
    for cp in px:
        cp.wait_recv()
    find(ppair_s, puser_s, pinv_s)
    for cp in spread_a[1::2] + spread_b[1::2] + near + fwd + pw:
        cp.wait_recv()
    for cp in tile_loads:
        cp.wait()

    def build(t, krao):
        s = slot_s[0, 0, 0, t]
        r = (s - i) & (NZ - 1)
        item32[...] = table[jnp.where(s < NZ, pos_s[r], NZ + r)].astype(F32)
        q = tword_s[0, 0, 0, t]
        word = words[pos_s[((q >> 1) - i) & (NZ - 1)], q & 1]
        for b in range(E):
            row = jnp.broadcast_to(item32[pl.ds(b, 1), :], (E, R)).astype(BF)
            krao[pl.ds(b * E, E), :] = row * word

    groups = ((0, 4), (4, 8))

    def send_tiles(n):
        lo, hi = groups[n]
        return pltpu.make_async_remote_copy(
            src_ref=contrib.at[pl.ds(lo, hi - lo)], dst_ref=pcontrib.at[pl.ds(lo, hi - lo)],
            send_sem=t_send.at[n], recv_sem=t_recv.at[n], device_id=other, device_id_type=MESH,
        )

    build(0, krao_a)
    for n, (lo, hi) in enumerate(groups):
        for t in range(lo, hi):
            now, later = (krao_a, krao_b) if t % 2 == 0 else (krao_b, krao_a)
            contrib[t] = jnp.dot(tiles[t], now[...], preferred_element_type=F32)
            if t + 1 < TILES:
                build(t + 1, later)
        send_tiles(n).start()
    for n in range(len(groups)):
        send_tiles(n).wait_recv()

    def plane(d):
        q = lax.rem(chip + d, 16)
        return q, pltpu.make_async_remote_copy(
            src_ref=plane_out.at[d], dst_ref=plane_in.at[d], send_sem=q_send.at[d], recv_sem=q_recv.at[d],
            device_id=chip_dev(q), device_id_type=MESH,
        )

    far_first = (10, 6, 14, 9, 11, 2, 8, 5, 7, 13, 15, 1, 3, 4, 12)
    for d in far_first:
        q, cp = plane(d)
        plane_out[d] = (contrib[inv_s[q]] + pcontrib[pinv_s[q]]).astype(BF)
        cp.start()
    total = contrib[inv_s[chip]] + pcontrib[pinv_s[chip]]
    for d in far_first[::-1]:
        plane(d)[1].wait_recv()
        total = total + plane_in[d].astype(F32)
    out_ref[0] = total

    for cp in list(ag.values()) + up + down + px + hops + near + spread_a + spread_b + fwd + pw:
        cp.wait_send()
    for n in range(len(groups)):
        send_tiles(n).wait_send()
    for d in far_first:
        plane(d)[1].wait_send()


def local(tiles, items, word_rows, heavy, send, slot, tword, user, count):
    dma = pltpu.SemaphoreType.DMA
    lane = lax.broadcasted_iota(jnp.int32, (1, R), 1)
    pair = jnp.where(lane == HEAVY, heavy.reshape(1, 1), count.reshape(1, 1))
    ints = (pair, send.reshape(1, 1, 1, NZ), slot, tword, user)
    args = [pltpu.with_memory_space_constraint(a, pltpu.HBM) for a in (tiles, items, word_rows, *ints)]
    return pl.pallas_call(
        kernel,
        out_shape=pltpu.VMEM((1, E, R), F32),
        in_specs=[pl.BlockSpec(memory_space=pltpu.HBM)] * 8,
        out_specs=pl.BlockSpec(memory_space=pltpu.VMEM),
        scratch_shapes=[
            pltpu.VMEM((TILES, E, E * E), BF),
            pltpu.VMEM((8, E, R), BF),
            pltpu.VMEM((NZ, 2, Q, R), BF),
            pltpu.VMEM((2 * NZ, E, R), BF),
            pltpu.VMEM((NZ, 2, E, R), BF),
            pltpu.VMEM((NZ, E, R), BF),
            pltpu.VMEM((2, 4, E, R), BF),
            pltpu.VMEM((E, R), F32),
            pltpu.VMEM((E * E, R), BF),
            pltpu.VMEM((E * E, R), BF),
            pltpu.VMEM((TILES + 1, E, R), F32),
            pltpu.VMEM((TILES + 1, E, R), F32),
            pltpu.VMEM((16, E, R), BF),
            pltpu.VMEM((16, E, R), BF),
            pltpu.SMEM((1, R), jnp.int32),
            pltpu.SMEM((1, 1, 1, NZ), jnp.int32),
            pltpu.SMEM((1, 1, 1, TILES), jnp.int32),
            pltpu.SMEM((1, 1, 1, TILES), jnp.int32),
            pltpu.SMEM((1, 1, 1, TILES), jnp.int32),
            pltpu.SMEM((1, R), jnp.int32),
            pltpu.SMEM((1, 1, 1, TILES), jnp.int32),
            pltpu.SMEM((16,), jnp.int32),
            pltpu.SMEM((16,), jnp.int32),
            pltpu.SMEM((16,), jnp.int32),
            dma((TILES,)), dma((7,)), dma((64,)), dma((64,)),
            dma((TILES,)), dma((TILES,)), dma((16,)), dma((16,)),
        ],
        compiler_params=pltpu.CompilerParams(collective_id=0, has_side_effects=True, vmem_limit_bytes=32 << 20),
        name="mttkrp",
    )(*args)


def solution(mesh):
    return jax.shard_map(
        local,
        mesh=mesh,
        in_specs=(
            P("ia", "ja", "ka", None, None, None),
            P(("ia", "ja"), None, None),
            P(("ia", "ka"), None, None),
            P("ia", "ja", None),
            P("ia", "ja", "ka", None, None),
            P("ia", "ja", "ka", None),
            P("ia", "ja", "ka", None),
            P("ia", "ja", "ka", None),
            P("ia", "ja", "ka"),
        ),
        out_specs=P(("ia", "ja", "ka"), None, None),
        check_vma=False,
    )
```

time: 56.7 us -> 46.7 us (0.82)
  local copies, waits for them, and re-layouts: 7.08 us -> 0.62 us
  Pallas kernels: 48 us -> 44.1 us
    unnamed x15 -> x1, local copies, waits for them, and re-layouts: 7.08 us -> 0.62 us
    pallas_call x1, Pallas kernels: 48 us -> 44.1 us  [local(): pl.pallas_call(kernel, out_shape=pltpu.VMEM((1, E, R), F32), in_specs=[pl...]
where the time goes in v2:
time: 46.7 us; the launch traced here: 46.6 us
  Pallas kernels  44.1 us (94%)
  between operations  1.31 us (3%)
  local copies, waits for them, and re-layouts  0.62 us (1%)
  other arithmetic  0.51 us (1%)
    pallas_call x1, Pallas kernels, local(): pl.pallas_call(kernel, out_shape=pltpu.VMEM((1, E, R), F32), in_specs=[pl...  44.1 us

profile of v2, /device:TPU:1, one launch (start us, length us, event | category | flops | bytes accessed | tf_op | source)
XLA Modules:
  0.0 46.6 jit_solution(16156009494304608285)
XLA Ops:
  1.3 0.5 %compare_select_fusion.pair_hbm = s32[1,128]{1,0:T(1,128)} fusion(s32[]{:T(128)} %bitcast.4, s32[]{:T(128)} %bitcast.3), kind=kLoop, calls=%fused_computation | loop fusion | flops 256 | bytes 520 | tf_op jit(solution)/shard_map/jit(_where)/select_n | solution.py:254
  1.8 44.1 %mttkrp.1 = f32[1,64,128]{2,1,0:T(8,128)S(1)} custom-call(bf16[1,1,1,8,64,4096]{5,4,3,2,1,0:T(8,128)(2,1)} %tiles_hbm.1, bf16[8,64,128]{2,1,0:T(8,128)(2,1)} %item_hbm.1, bf16[2,64,128]{2,1,0:T(8,128)(2,1)} %word_hbm.1, s32[1,128]{1,0:T(1,128)} %compare_select_fusion.pair_hbm, s32[1,1,1,16]{3,2,1,0:T(1,128)} %bitcast.5, s32[1,1,1,8]{3,2,1,0:T(1,128)} %slot_hbm.1, ...), custom_call_target="tpu_custom_call" | custom-call | tf_op jit(solution)/shard_map/mttkrp/pallas_call | solution.py:257
  45.9 0.6 %copy.11 = f32[1,64,128]{2,1,0:T(8,128)} copy(f32[1,64,128]{2,1,0:T(8,128)S(1)} %mttkrp.1) | data formatting | bytes 65536

commit v3 on v2

--- a/solution.py
+++ b/solution.py
@@ -18,14 +18,13 @@
 FAR = (3, 13, 5, 11, 6, 10, 7, 9, 8)
 POS = {r: n for n, r in enumerate(NEAR + FAR)}
 SPLIT = len(NEAR)
-HEAVY, COUNT = 0, 1
 
 
 def kernel(
-    tiles_hbm, item_hbm, word_hbm, pair_hbm, send_hbm, slot_hbm, tword_hbm, user_hbm,
+    tiles_hbm, item_hbm, word_hbm, send_hbm, slot_hbm, tword_hbm, user_hbm, heavy_s, count_s,
     out_ref,
     tiles, items, gath, table, words, light, relay, item32, krao_a, krao_b, contrib, pcontrib, plane_out, plane_in,
-    pair_s, send_s, slot_s, tword_s, user_s, ppair_s, puser_s, pos_s, inv_s, pinv_s,
+    send_s, slot_s, tword_s, user_s, pcount_s, puser_s, pos_s, inv_s, pinv_s,
     tile_sem, load_sem, ss, rs, t_send, t_recv, q_send, q_recv,
 ):
     i = lax.axis_index("ia")
@@ -55,7 +54,7 @@
 
     load_items = pltpu.make_async_copy(item_hbm, items, load_sem.at[0])
     load_word = pltpu.make_async_copy(word_hbm.at[c, pl.ds(yq, Q)], gath.at[0, 1], load_sem.at[1])
-    ints = ((pair_hbm, pair_s), (send_hbm, send_s), (slot_hbm, slot_s), (tword_hbm, tword_s), (user_hbm, user_s))
+    ints = ((send_hbm, send_s), (slot_hbm, slot_s), (tword_hbm, tword_s), (user_hbm, user_s))
     ints = [pltpu.make_async_copy(a, b, load_sem.at[2 + n]) for n, (a, b) in enumerate(ints)]
     for cp in ints:
         cp.start()
@@ -79,13 +78,13 @@
         cp.wait()
     load_items.wait()
     load_word.wait()
-    gath[0, 0] = items[pair_s[0, HEAVY], pl.ds(kq, Q), :]
+    gath[0, 0] = items[heavy_s[0, 0, 0], pl.ds(kq, Q), :]
     for d in range(1, NZ):
         light[d] = items[send_s[0, 0, 0, lax.rem(i + d, NZ)]]
     table[NZ] = items[send_s[0, 0, 0, i]]
 
-    def find(pair, user, inv):
-        count = pair[0, COUNT]
+    def find(live, user, inv):
+        count = live[0, 0, 0]
 
         def body(n, carry):
             u = (n // NX) * (NC * NX) + c * NX + lax.rem(n, NX)
@@ -97,9 +96,6 @@
 
         lax.fori_loop(0, NX * NY, body, 0)
 
-    find(pair_s, user_s, inv_s)
-    contrib[TILES] = jnp.zeros((E, R), F32)
-    pcontrib[TILES] = jnp.zeros((E, R), F32)
 
     pl.semaphore_wait(barrier, 24)
 
@@ -118,9 +114,12 @@
     for a, b in zip(up, down):
         a.start()
         b.start()
-    px = [remote(pair_hbm, ppair_s, other), remote(user_hbm, puser_s, other)]
+    px = [remote(count_s, pcount_s, other), remote(user_hbm, puser_s, other)]
     for cp in px:
         cp.start()
+    find(count_s, user_s, inv_s)
+    contrib[TILES] = jnp.zeros((E, R), F32)
+    pcontrib[TILES] = jnp.zeros((E, R), F32)
 
     ag[12].wait_recv()
     ag[4].wait_recv()
@@ -186,7 +185,7 @@
     pw = [pair_words(spread_a, 0, SPLIT), pair_words(spread_b, SPLIT, NZ - SPLIT)]
     for cp in px:
         cp.wait_recv()
-    find(ppair_s, puser_s, pinv_s)
+    find(pcount_s, puser_s, pinv_s)
     for cp in spread_a[1::2] + spread_b[1::2] + near + fwd + pw:
         cp.wait_recv()
     for cp in tile_loads:
@@ -222,42 +221,45 @@
     for n in range(len(groups)):
         send_tiles(n).wait_recv()
 
-    def plane(d):
-        q = lax.rem(chip + d, 16)
-        return q, pltpu.make_async_remote_copy(
-            src_ref=plane_out.at[d], dst_ref=plane_in.at[d], send_sem=q_send.at[d], recv_sem=q_recv.at[d],
+    def plane(dy, dx):
+        q = lax.rem(y + dy, NY) * NX + lax.rem(k + dx, NX)
+        n = dy * NX + dx
+        return n, q, pltpu.make_async_remote_copy(
+            src_ref=plane_out.at[n], dst_ref=plane_in.at[n], send_sem=q_send.at[n], recv_sem=q_recv.at[n],
             device_id=chip_dev(q), device_id_type=MESH,
         )
 
-    far_first = (10, 6, 14, 9, 11, 2, 8, 5, 7, 13, 15, 1, 3, 4, 12)
-    for d in far_first:
-        q, cp = plane(d)
-        plane_out[d] = (contrib[inv_s[q]] + pcontrib[pinv_s[q]]).astype(BF)
+    far_first = (
+        (2, 2), (2, 1), (2, 3), (1, 2), (3, 2), (1, 1), (3, 3), (1, 3), (3, 1), (2, 0), (0, 2), (1, 0), (3, 0), (0, 1), (0, 3),
+    )
+    for at in far_first:
+        n, q, cp = plane(*at)
+        plane_out[n] = (contrib[inv_s[q]] + pcontrib[pinv_s[q]]).astype(BF)
         cp.start()
     total = contrib[inv_s[chip]] + pcontrib[pinv_s[chip]]
-    for d in far_first[::-1]:
-        plane(d)[1].wait_recv()
-        total = total + plane_in[d].astype(F32)
+    for at in far_first[::-1]:
+        n, _, cp = plane(*at)
+        cp.wait_recv()
+        total = total + plane_in[n].astype(F32)
     out_ref[0] = total
 
     for cp in list(ag.values()) + up + down + px + hops + near + spread_a + spread_b + fwd + pw:
         cp.wait_send()
     for n in range(len(groups)):
         send_tiles(n).wait_send()
-    for d in far_first:
-        plane(d)[1].wait_send()
+    for at in far_first:
+        plane(*at)[2].wait_send()
 
 
 def local(tiles, items, word_rows, heavy, send, slot, tword, user, count):
     dma = pltpu.SemaphoreType.DMA
-    lane = lax.broadcasted_iota(jnp.int32, (1, R), 1)
-    pair = jnp.where(lane == HEAVY, heavy.reshape(1, 1), count.reshape(1, 1))
-    ints = (pair, send.reshape(1, 1, 1, NZ), slot, tword, user)
+    ints = (send.reshape(1, 1, 1, NZ), slot, tword, user)
     args = [pltpu.with_memory_space_constraint(a, pltpu.HBM) for a in (tiles, items, word_rows, *ints)]
+    args += [heavy, count]
     return pl.pallas_call(
         kernel,
         out_shape=pltpu.VMEM((1, E, R), F32),
-        in_specs=[pl.BlockSpec(memory_space=pltpu.HBM)] * 8,
+        in_specs=[pl.BlockSpec(memory_space=pltpu.HBM)] * 7 + [pl.BlockSpec(memory_space=pltpu.SMEM)] * 2,
         out_specs=pl.BlockSpec(memory_space=pltpu.VMEM),
         scratch_shapes=[
             pltpu.VMEM((TILES, E, E * E), BF),
@@ -274,17 +276,16 @@
             pltpu.VMEM((TILES + 1, E, R), F32),
             pltpu.VMEM((16, E, R), BF),
             pltpu.VMEM((16, E, R), BF),
-            pltpu.SMEM((1, R), jnp.int32),
             pltpu.SMEM((1, 1, 1, NZ), jnp.int32),
             pltpu.SMEM((1, 1, 1, TILES), jnp.int32),
             pltpu.SMEM((1, 1, 1, TILES), jnp.int32),
             pltpu.SMEM((1, 1, 1, TILES), jnp.int32),
-            pltpu.SMEM((1, R), jnp.int32),
+            pltpu.SMEM((1, 1, 1), jnp.int32),
             pltpu.SMEM((1, 1, 1, TILES), jnp.int32),
             pltpu.SMEM((16,), jnp.int32),
             pltpu.SMEM((16,), jnp.int32),
             pltpu.SMEM((16,), jnp.int32),
-            dma((TILES,)), dma((7,)), dma((64,)), dma((64,)),
+            dma((TILES,)), dma((6,)), dma((64,)), dma((64,)),
             dma((TILES,)), dma((TILES,)), dma((16,)), dma((16,)),
         ],
         compiler_params=pltpu.CompilerParams(collective_id=0, has_side_effects=True, vmem_limit_bytes=32 << 20),

time: 46.7 us -> 45 us (0.964)
  Pallas kernels: 44.1 us -> 42.8 us
  other arithmetic: 0.51 us -> 0 us
    pallas_call x1, Pallas kernels: 44.1 us -> 42.8 us  [local(): pl.pallas_call(kernel, out_shape=pltpu.VMEM((1, E, R), F32), in_specs=[pl...]
    select_n x1 -> x0, other arithmetic: 0.51 us -> none  [local(): pair = jnp.where(lane == HEAVY, heavy.reshape(1, 1), count.reshape(1, 1))]
where the time goes in v3:
time: 45 us; the launch traced here: 44.7 us
  Pallas kernels  42.8 us (95%)
  between operations  1.3 us (3%)
  local copies, waits for them, and re-layouts  0.62 us (1%)
    pallas_call x1, Pallas kernels, local(): pl.pallas_call(kernel, out_shape=pltpu.VMEM((1, E, R), F32), in_specs=[pl...  42.8 us

profile of v3, /device:TPU:1, one launch (start us, length us, event | category | flops | bytes accessed | tf_op | source)
XLA Modules:
  0.0 44.7 jit_solution(7776562062886606604)
XLA Ops:
  1.3 42.8 %mttkrp.1 = f32[1,64,128]{2,1,0:T(8,128)S(1)} custom-call(bf16[1,1,1,8,64,4096]{5,4,3,2,1,0:T(8,128)(2,1)} %tiles_hbm.1, bf16[8,64,128]{2,1,0:T(8,128)(2,1)} %item_hbm.1, bf16[2,64,128]{2,1,0:T(8,128)(2,1)} %word_hbm.1, s32[1,1,1,16]{3,2,1,0:T(1,128)} %bitcast.1, s32[1,1,1,8]{3,2,1,0:T(1,128)} %slot_hbm.1, s32[1,1,1,8]{3,2,1,0:T(1,128)} %tword_hbm.1, ...), custom_call_target="tpu_custom_call" | custom-call | tf_op jit(solution)/shard_map/mttkrp/pallas_call | solution.py:259
  44.1 0.6 %copy.11 = f32[1,64,128]{2,1,0:T(8,128)} copy(f32[1,64,128]{2,1,0:T(8,128)S(1)} %mttkrp.1) | data formatting | bytes 65536

commit v4 on v3

--- a/solution.py
+++ b/solution.py
@@ -18,6 +18,9 @@
 FAR = (3, 13, 5, 11, 6, 10, 7, 9, 8)
 POS = {r: n for n, r in enumerate(NEAR + FAR)}
 SPLIT = len(NEAR)
+PLANE = (
+    (2, 2), (2, 1), (2, 3), (1, 2), (3, 2), (1, 1), (3, 3), (1, 3), (3, 1), (2, 0), (0, 2), (1, 0), (3, 0), (0, 1), (0, 3),
+)
 
 
 def kernel(
@@ -54,19 +57,26 @@
 
     load_items = pltpu.make_async_copy(item_hbm, items, load_sem.at[0])
     load_word = pltpu.make_async_copy(word_hbm.at[c, pl.ds(yq, Q)], gath.at[0, 1], load_sem.at[1])
+    barrier = pltpu.get_barrier_semaphore()
+
+    def greet(device):
+        pl.semaphore_signal(barrier, inc=1, device_id=device, device_id_type=MESH)
+
+    greet(zdev(4))
+    greet(zdev(-4))
+    for n, (dy, dx) in enumerate(PLANE):
+        greet(chip_dev(lax.rem(y + dy, NY) * NX + lax.rem(k + dx, NX)))
+        if n in (0, 4, 8):
+            greet(zdev(3 - n // 4))
+            greet(zdev(n // 4 - 3))
+    greet(other)
+
     ints = ((send_hbm, send_s), (slot_hbm, slot_s), (tword_hbm, tword_s), (user_hbm, user_s))
     ints = [pltpu.make_async_copy(a, b, load_sem.at[2 + n]) for n, (a, b) in enumerate(ints)]
     for cp in ints:
         cp.start()
     load_items.start()
     load_word.start()
-
-    barrier = pltpu.get_barrier_semaphore()
-    for d in (4, -4, 3, -3, 2, -2, 1, -1):
-        pl.semaphore_signal(barrier, inc=1, device_id=zdev(d), device_id_type=MESH)
-    for d in range(1, 16):
-        pl.semaphore_signal(barrier, inc=1, device_id=chip_dev(lax.rem(chip + d, 16)), device_id_type=MESH)
-    pl.semaphore_signal(barrier, inc=1, device_id=other, device_id_type=MESH)
 
     tile_loads = [pltpu.make_async_copy(tiles_hbm.at[0, 0, 0, t], tiles.at[t], tile_sem.at[t]) for t in range(TILES)]
     for cp in tile_loads:
@@ -229,15 +239,12 @@
             device_id=chip_dev(q), device_id_type=MESH,
         )
 
-    far_first = (
-        (2, 2), (2, 1), (2, 3), (1, 2), (3, 2), (1, 1), (3, 3), (1, 3), (3, 1), (2, 0), (0, 2), (1, 0), (3, 0), (0, 1), (0, 3),
-    )
-    for at in far_first:
+    for at in PLANE:
         n, q, cp = plane(*at)
         plane_out[n] = (contrib[inv_s[q]] + pcontrib[pinv_s[q]]).astype(BF)
         cp.start()
     total = contrib[inv_s[chip]] + pcontrib[pinv_s[chip]]
-    for at in far_first[::-1]:
+    for at in PLANE[::-1]:
         n, _, cp = plane(*at)
         cp.wait_recv()
         total = total + plane_in[n].astype(F32)
@@ -247,7 +254,7 @@
         cp.wait_send()
     for n in range(len(groups)):
         send_tiles(n).wait_send()
-    for at in far_first:
+    for at in PLANE:
         plane(*at)[2].wait_send()
 
 

time: 45 us -> 45.1 us (level)
  no operation moved by 1% of the time
where the time goes in v4:
time: 45.1 us; the launch traced here: 45 us
  Pallas kernels  43.1 us (96%)
  between operations  1.3 us (3%)
  local copies, waits for them, and re-layouts  0.62 us (1%)
    pallas_call x1, Pallas kernels, local(): pl.pallas_call(kernel, out_shape=pltpu.VMEM((1, E, R), F32), in_specs=[pl...  43.1 us

profile of v4, /device:TPU:1, one launch (start us, length us, event | category | flops | bytes accessed | tf_op | source)
XLA Modules:
  0.0 45.0 jit_solution(1528719533221241542)
XLA Ops:
  1.3 43.1 %mttkrp.1 = f32[1,64,128]{2,1,0:T(8,128)S(1)} custom-call(bf16[1,1,1,8,64,4096]{5,4,3,2,1,0:T(8,128)(2,1)} %tiles_hbm.1, bf16[8,64,128]{2,1,0:T(8,128)(2,1)} %item_hbm.1, bf16[2,64,128]{2,1,0:T(8,128)(2,1)} %word_hbm.1, s32[1,1,1,16]{3,2,1,0:T(1,128)} %bitcast.1, s32[1,1,1,8]{3,2,1,0:T(1,128)} %slot_hbm.1, s32[1,1,1,8]{3,2,1,0:T(1,128)} %tword_hbm.1, ...), custom_call_target="tpu_custom_call" | custom-call | tf_op jit(solution)/shard_map/mttkrp/pallas_call | solution.py:266
  44.4 0.6 %copy.11 = f32[1,64,128]{2,1,0:T(8,128)} copy(f32[1,64,128]{2,1,0:T(8,128)S(1)} %mttkrp.1) | data formatting | bytes 65536

commit v5 on v4

--- a/solution.py
+++ b/solution.py
@@ -121,7 +121,7 @@
     for f in (3, 2, 1):
         up.append(remote(light.at[4 + f], relay.at[0, f - 1], zdev(4)))
         down.append(remote(light.at[NZ - 4 - f], relay.at[1, f - 1], zdev(-4)))
-    for a, b in zip(up, down):
+    for a, b in zip(up[:2], down[:2]):
         a.start()
         b.start()
     px = [remote(count_s, pcount_s, other), remote(user_hbm, puser_s, other)]
@@ -145,6 +145,9 @@
     for cp in hops:
         cp.start()
 
+    for a, b in zip(up[2:], down[2:]):
+        a.start()
+        b.start()
     near = [remote(light.at[d % NZ], table.at[NZ + (-d % NZ)], zdev(d)) for d in (4, -4, 3, -3, 2, -2, 1, -1)]
     for cp in near:
         cp.start()

time: 45.1 us -> 47.1 us (1.044)
  Pallas kernels: 43.1 us -> 45 us
    pallas_call x1, Pallas kernels: 43.1 us -> 45 us  [local(): pl.pallas_call(kernel, out_shape=pltpu.VMEM((1, E, R), F32), in_specs=[pl...]
where the time goes in v5:
time: 47.1 us; the launch traced here: 46.9 us
  Pallas kernels  45 us (96%)
  between operations  1.3 us (3%)
  local copies, waits for them, and re-layouts  0.62 us (1%)
    pallas_call x1, Pallas kernels, local(): pl.pallas_call(kernel, out_shape=pltpu.VMEM((1, E, R), F32), in_specs=[pl...  45 us

profile of v5, /device:TPU:1, one launch (start us, length us, event | category | flops | bytes accessed | tf_op | source)
XLA Modules:
  0.0 46.9 jit_solution(18434940111791833800)
XLA Ops:
  1.3 45.0 %mttkrp.1 = f32[1,64,128]{2,1,0:T(8,128)S(1)} custom-call(bf16[1,1,1,8,64,4096]{5,4,3,2,1,0:T(8,128)(2,1)} %tiles_hbm.1, bf16[8,64,128]{2,1,0:T(8,128)(2,1)} %item_hbm.1, bf16[2,64,128]{2,1,0:T(8,128)(2,1)} %word_hbm.1, s32[1,1,1,16]{3,2,1,0:T(1,128)} %bitcast.1, s32[1,1,1,8]{3,2,1,0:T(1,128)} %slot_hbm.1, s32[1,1,1,8]{3,2,1,0:T(1,128)} %tword_hbm.1, ...), custom_call_target="tpu_custom_call" | custom-call | tf_op jit(solution)/shard_map/mttkrp/pallas_call | solution.py:269
  46.3 0.6 %copy.11 = f32[1,64,128]{2,1,0:T(8,128)} copy(f32[1,64,128]{2,1,0:T(8,128)S(1)} %mttkrp.1) | data formatting | bytes 65536
